TPU v7x, 32 devices: a whole 2x2x4 slice. The times are simulated.
32 devices in a mesh: row: 4 (over x, core), col: 8 (over z, y).
Axes of the slice: x: 2, y: 2, z: 4, core: 2. Of those that a mesh axis runs over, the one named last changes fastest.
Arguments:
- panel: float32 [6, 2048, 2048], P(None, 'row', 'col'), may hold values from -0.0625 to 0.0625
- inverse_blocks: float32 [4, 2048, 2048], P(None, 'row', 'col'), may hold values from -1.5 to 1.5, as said below
- trailing_factor: float32 [12, 2048, 4, 2048], P(None, 'row', None, 'col'), may hold values from -0.0625 to 0.0625
- columns: float32 [4, 2048, 1024], P(None, 'row', 'col'), may hold values from -6 to 6
- trailing_columns: float32 [12, 2048, 1024], P(None, 'row', 'col'), may hold values from -6 to 6
Outputs:
- whitened: float32 [4, 2048, 1024], P(None, 'row', 'col')
- updated: float32 [12, 2048, 1024], P(None, 'row', 'col')
- variance_drop: float32 [1024], P('col')
Inputs may be any that keep to these rules, and one draw needn't show every extreme that they name: `inverse_blocks`: each block is lower triangular; its diagonal entries lie between 0.5 and 1.5.
All inputs are finite; a program needn't handle non-finite values.
Results may differ from a plain program's by a relative error of at most 0.00011.
Values sent between devices are 32-bit elements; how exact they have to be, the bound alone decides.
A program may use at most 128 MiB of HBM per device.

v0:
```python
import jax
import jax.numpy as jnp
from jax import lax
from jax.sharding import PartitionSpec as P


def product(left, right):
    return jnp.dot(left, right, precision=lax.Precision.HIGHEST, preferred_element_type=jnp.float32)


def remap(block):
    full = lax.all_gather(block, "row", axis=0, tiled=True)
    spread = lax.all_to_all(full, "col", split_axis=0, concat_axis=1, tiled=True)
    return (full, spread)


def shards(panel, inverse_blocks, trailing_factor, columns, trailing_columns):
    steps = columns.shape[0]
    order = columns.shape[1] * lax.axis_size("row")
    solved = []
    fulls = []
    spreads = []
    for j in range(steps):
        reduced = columns[j]
        if j > 0:
            partial_value = product(panel[j * (j - 1) // 2], spreads[0])
            for i in range(1, j):
                partial_value = partial_value + product(panel[j * (j - 1) // 2 + i], spreads[i])
            reduced = reduced - lax.psum_scatter(
                partial_value, "col", scatter_dimension=1, tiled=True
            )
        unused, reduced_spread = remap(reduced)
        result = lax.psum_scatter(
            product(inverse_blocks[j], reduced_spread), "col", scatter_dimension=1, tiled=True
        )
        full, spread = remap(result)
        solved.append(result)
        fulls.append(full)
        spreads.append(spread)
    whitened = jnp.stack(solved)
    stacked = jnp.stack(spreads)
    summed = lax.psum_scatter(
        jnp.einsum(
            "tajb,jbm->mta",
            trailing_factor,
            stacked,
            precision=lax.Precision.HIGHEST,
            preferred_element_type=jnp.float32,
        ),
        "col",
        scatter_dimension=0,
        tiled=True,
    )
    updated = trailing_columns - jnp.transpose(summed, (1, 2, 0))
    local_squares = jnp.sum(whitened * whitened, axis=(0, 1))
    variance_drop = lax.psum(local_squares, "row") / (steps * order)
    return (whitened, updated, variance_drop)


def solution(mesh):
    return jax.shard_map(
        shards,
        mesh=mesh,
        in_specs=(
            P(None, "row", "col"),
            P(None, "row", "col"),
            P(None, "row", None, "col"),
            P(None, "row", "col"),
            P(None, "row", "col"),
        ),
        out_specs=(P(None, "row", "col"), P(None, "row", "col"), P("col")),
        check_vma=False,
    )
```

profile of v0, /device:TPU:0, one launch (start us, length us, event | category | flops | bytes accessed | tf_op | source)
XLA Modules:
  0.0 1418.2 jit_solution(50146526596342882)
XLA Ops:
  9.3 20.3 %all-gather.24.cloned.1.call-done = f32[1,2048,128]{2,1,0:T(8,128)} async-done(((f32[1,512,128]{2,1,0:T(8,128)}), f32[1,2048,128]{2,1,0:T(8,128)}) %all-gather.24.cloned.1.call-update) | async-done | bytes 1048592 | tf_op jit(solution)/shard_map/all_gather | solution.py:12
  29.6 31.6 %all_to_all.149 = f32[8,256,128]{2,1,0:T(8,128)S(1)} all-to-all(f32[8,256,128]{2,1,0:T(8,128)} %bitcast.140), channel_id=1, replica_groups=mesh['row'=4,'col'=8] {'col'}, dimensions={0} | all-to-all | bytes 2097152 | tf_op jit(solution)/shard_map/all_to_all | solution.py:13
  61.6 4.2 fusion.23
  65.9 66.5 %reduce-scatter.9.cloned.1.call-done = f32[512,128]{1,0:T(8,128)} async-done(((f32[512,1024]{1,0:T(8,128)}), f32[512,128]{1,0:T(8,128)}) %reduce-scatter.9.cloned.1.call-update) | async-done | bytes 262160 | tf_op jit(solution)/shard_map/reduce_scatter | solution.py:33
  132.4 17.3 %all-gather.10.cloned.1.call-done = f32[2048,128]{1,0:T(8,128)} async-done(((f32[512,128]{1,0:T(8,128)}), f32[2048,128]{1,0:T(8,128)}) %all-gather.10.cloned.1.call-update) | async-done | bytes 1048592 | tf_op jit(solution)/shard_map/all_gather | solution.py:12
  151.2 31.4 %all_to_all.150 = f32[8,256,128]{1,2,0:T(8,128)S(1)} all-to-all(f32[8,256,128]{1,2,0:T(8,128)S(1)} %copy.39), channel_id=1, replica_groups=mesh['row'=4,'col'=8] {'col'}, dimensions={0} | all-to-all | bytes 2097152 | tf_op jit(solution)/shard_map/all_to_all | solution.py:13
  187.1 66.0 %reduce-scatter.11.cloned.1.call-done = f32[512,128]{0,1:T(8,128)} async-done(((f32[512,1024]{0,1:T(8,128)}), f32[512,128]{0,1:T(8,128)}) %reduce-scatter.11.cloned.1.call-update) | async-done | bytes 262160 | tf_op jit(solution)/shard_map/reduce_scatter | solution.py:29
  254.8 16.0 %all-gather.12.cloned.1.call-done = f32[2048,128]{0,1:T(8,128)} async-done(((f32[512,128]{0,1:T(8,128)}), f32[2048,128]{0,1:T(8,128)}) %all-gather.12.cloned.1.call-update) | async-done | bytes 1048592 | tf_op jit(solution)/shard_map/all_gather | solution.py:12
  272.1 31.4 %all_to_all.151 = f32[8,256,128]{1,2,0:T(8,128)S(1)} all-to-all(f32[8,256,128]{1,2,0:T(8,128)S(1)} %bitcast.132), channel_id=1, replica_groups=mesh['row'=4,'col'=8] {'col'}, dimensions={0} | all-to-all | bytes 2097152 | tf_op jit(solution)/shard_map/all_to_all | solution.py:13
  307.9 66.2 %reduce-scatter.13.cloned.1.call-done = f32[512,128]{1,0:T(8,128)} async-done(((f32[512,1024]{1,0:T(8,128)}), f32[512,128]{1,0:T(8,128)}) %reduce-scatter.13.cloned.1.call-update) | async-done | bytes 262160 | tf_op jit(solution)/shard_map/reduce_scatter | solution.py:33
  374.1 17.4 %all-gather.14.cloned.1.call-done = f32[2048,128]{1,0:T(8,128)} async-done(((f32[512,128]{1,0:T(8,128)}), f32[2048,128]{1,0:T(8,128)}) %all-gather.14.cloned.1.call-update) | async-done | bytes 1048592 | tf_op jit(solution)/shard_map/all_gather | solution.py:12
  394.0 5.5 all-to-all-start.3
  404.0 21.7 %all-to-all-done.3 = f32[8,256,128]{1,2,0:T(8,128)S(1)} async-done(((f32[8,256,128]{1,2,0:T(8,128)}), f32[8,256,128]{1,2,0:T(8,128)S(1)}, u32[]{:S(2)}, u32[]{:S(2)}) %all-to-all-start.3) | async-done | bytes 1048608 | tf_op jit(solution)/shard_map/all_to_all | solution.py:13
  425.7 4.9 add_bitcast_fusion.1
  430.9 65.8 %reduce-scatter.15.cloned.1.call-done = f32[512,128]{0,1:T(8,128)} async-done(((f32[512,1024]{0,1:T(8,128)}), f32[512,128]{0,1:T(8,128)}) %reduce-scatter.15.cloned.1.call-update) | async-done | bytes 262160 | tf_op jit(solution)/shard_map/reduce_scatter | solution.py:29
  498.4 16.2 %all-gather.16.cloned.1.call-done = f32[2048,128]{0,1:T(8,128)} async-done(((f32[512,128]{0,1:T(8,128)}), f32[2048,128]{0,1:T(8,128)}) %all-gather.16.cloned.1.call-update) | async-done | bytes 1048592 | tf_op jit(solution)/shard_map/all_gather | solution.py:12
  515.9 31.4 %all_to_all.152 = f32[8,256,128]{1,2,0:T(8,128)S(1)} all-to-all(f32[8,256,128]{1,2,0:T(8,128)S(1)} %bitcast.133), channel_id=1, replica_groups=mesh['row'=4,'col'=8] {'col'}, dimensions={0} | all-to-all | bytes 2097152 | tf_op jit(solution)/shard_map/all_to_all | solution.py:13
  551.7 66.3 %reduce-scatter.17.cloned.1.call-done = f32[512,128]{1,0:T(8,128)} async-done(((f32[512,1024]{1,0:T(8,128)}), f32[512,128]{1,0:T(8,128)}) %reduce-scatter.17.cloned.1.call-update) | async-done | bytes 262160 | tf_op jit(solution)/shard_map/reduce_scatter | solution.py:33
  618.0 17.3 %all-gather.18.cloned.1.call-done = f32[2048,128]{1,0:T(8,128)} async-done(((f32[512,128]{1,0:T(8,128)}), f32[2048,128]{1,0:T(8,128)}) %all-gather.18.cloned.1.call-update) | async-done | bytes 1048592 | tf_op jit(solution)/shard_map/all_gather | solution.py:12
  637.8 5.5 all-to-all-start.5
  652.0 17.5 %all-to-all-done.5 = f32[8,256,128]{1,2,0:T(8,128)S(1)} async-done(((f32[8,256,128]{1,2,0:T(8,128)}), f32[8,256,128]{1,2,0:T(8,128)S(1)}, u32[]{:S(2)}, u32[]{:S(2)}) %all-to-all-start.5) | async-done | bytes 1048608 | tf_op jit(solution)/shard_map/all_to_all | solution.py:13
  669.5 5.6 add_bitcast_fusion
  676.3 64.9 %reduce-scatter.19.cloned.1.call-done = f32[512,128]{0,1:T(8,128)} async-done(((f32[512,1024]{0,1:T(8,128)}), f32[512,128]{0,1:T(8,128)}) %reduce-scatter.19.cloned.1.call-update) | async-done | bytes 262160 | tf_op jit(solution)/shard_map/reduce_scatter | solution.py:29
  742.9 16.2 %all-gather.20.cloned.1.call-done = f32[2048,128]{0,1:T(8,128)} async-done(((f32[512,128]{0,1:T(8,128)}), f32[2048,128]{0,1:T(8,128)}) %all-gather.20.cloned.1.call-update) | async-done | bytes 1048592 | tf_op jit(solution)/shard_map/all_gather | solution.py:12
  760.4 31.4 %all_to_all.153 = f32[8,256,128]{1,2,0:T(8,128)S(1)} all-to-all(f32[8,256,128]{1,2,0:T(8,128)S(1)} %bitcast.134), channel_id=1, replica_groups=mesh['row'=4,'col'=8] {'col'}, dimensions={0} | all-to-all | bytes 2097152 | tf_op jit(solution)/shard_map/all_to_all | solution.py:13
  796.1 66.3 %reduce-scatter.21.cloned.1.call-done = f32[512,128]{1,0:T(8,128)} async-done(((f32[512,1024]{1,0:T(8,128)}), f32[512,128]{1,0:T(8,128)}) %reduce-scatter.21.cloned.1.call-update) | async-done | bytes 262160 | tf_op jit(solution)/shard_map/reduce_scatter | solution.py:33
  862.5 17.1 %all-gather.22.cloned.1.call-done = f32[2048,128]{1,0:T(8,128)} async-done(((f32[512,128]{1,0:T(8,128)}), f32[2048,128]{1,0:T(8,128)}) %all-gather.22.cloned.1.call-update) | async-done | bytes 1048592 | tf_op jit(solution)/shard_map/all_gather | solution.py:12
  879.6 31.7 %all_to_all.154 = f32[8,256,128]{2,1,0:T(8,128)} all-to-all(f32[8,256,128]{2,1,0:T(8,128)} %bitcast.145), channel_id=1, replica_groups=mesh['row'=4,'col'=8] {'col'}, dimensions={0} | all-to-all | bytes 2097152 | tf_op jit(solution)/shard_map/all_to_all | solution.py:13
  913.8 86.8 %fusion.2 = f32[1024,12,512]{2,0,1:T(8,128)} fusion(f32[12,512,4,256]{3,2,1,0:T(4,128)} %param.7, f32[1,256,1024]{1,2,0:T(8,128)} %bitcast.148, f32[1,256,1024]{1,2,0:T(8,128)S(1)} %bitcast.126, f32[1,256,1024]{1,2,0:T(8,128)S(1)} %bitcast.124, f32[1,256,1024]{1,2,0:T(8,128)S(1)} %bitcast.121), kind=kOutput, calls=%fused_computation.2 | convolution fusion | flops 77312557056 | bytes 54525952 | tf_op jit(solution)/shard_map/tajb,jbm->mta/dot_general | solution.py:43
  1005.4 6.0 psum.7
  1012.0 391.5 %reduce-scatter.23.cloned.1.call-done = f32[128,12,512]{2,0,1:T(8,128)} async-done(((f32[1024,12,512]{2,0,1:T(8,128)}), f32[128,12,512]{2,0,1:T(8,128)}) %reduce-scatter.23.cloned.1.call-update) | async-done | bytes 3145744 | tf_op jit(solution)/shard_map/reduce_scatter | solution.py:42
  1403.5 4.3 bitcast_subtract_fusion
  (60 shorter events, 61.4 us)
Async XLA Ops:
  7.2 22.4 %all-gather.24.cloned.1.call-start = ((), (), s32[]{:S(2)}) async-start(), calls=%async_computation.31 | async-start | bytes 1310720 | tf_op jit(solution)/shard_map/all_gather | solution.py:12
  9.3 123.1 %reduce-scatter.9.cloned.1.call-start = ((), (), s32[]{:S(2)}) async-start(), calls=%async_computation.16 | async-start | bytes 2359296 | tf_op jit(solution)/shard_map/reduce_scatter | solution.py:33
  65.8 83.9 %all-gather.10.cloned.1.call-start = ((), (), s32[]{:S(2)}) async-start(), calls=%async_computation.17 | async-start | bytes 1310720 | tf_op jit(solution)/shard_map/all_gather | solution.py:12
  132.4 120.7 %reduce-scatter.11.cloned.1.call-start = ((), (), s32[]{:S(2)}) async-start(), calls=%async_computation.18 | async-start | bytes 2359296 | tf_op jit(solution)/shard_map/reduce_scatter | solution.py:29
  186.9 83.9 %all-gather.12.cloned.1.call-start = ((), (), s32[]{:S(2)}) async-start(), calls=%async_computation.19 | async-start | bytes 1310720 | tf_op jit(solution)/shard_map/all_gather | solution.py:12
  254.8 119.3 %reduce-scatter.13.cloned.1.call-start = ((), (), s32[]{:S(2)}) async-start(), calls=%async_computation.20 | async-start | bytes 2359296 | tf_op jit(solution)/shard_map/reduce_scatter | solution.py:33
  307.8 83.7 %all-gather.14.cloned.1.call-start = ((), (), s32[]{:S(2)}) async-start(), calls=%async_computation.21 | async-start | bytes 1310720 | tf_op jit(solution)/shard_map/all_gather | solution.py:12
  394.0 31.7 %all-to-all-start.3 = ((f32[8,256,128]{1,2,0:T(8,128)}), f32[8,256,128]{1,2,0:T(8,128)S(1)}, u32[]{:S(2)}, u32[]{:S(2)}) async-start(f32[8,256,128]{1,2,0:T(8,128)} %copy.43), calls=%async_computation.6 | async-start | bytes 2097152 | tf_op jit(solution)/shard_map/all_to_all | solution.py:13
  399.6 97.1 %reduce-scatter.15.cloned.1.call-start = ((), (), s32[]{:S(2)}) async-start(), calls=%async_computation.22 | async-start | bytes 2359296 | tf_op jit(solution)/shard_map/reduce_scatter | solution.py:29
  430.7 83.9 %all-gather.16.cloned.1.call-start = ((), (), s32[]{:S(2)}) async-start(), calls=%async_computation.23 | async-start | bytes 1310720 | tf_op jit(solution)/shard_map/all_gather | solution.py:12
  498.4 119.6 %reduce-scatter.17.cloned.1.call-start = ((), (), s32[]{:S(2)}) async-start(), calls=%async_computation.24 | async-start | bytes 2359296 | tf_op jit(solution)/shard_map/reduce_scatter | solution.py:33
  551.6 83.7 %all-gather.18.cloned.1.call-start = ((), (), s32[]{:S(2)}) async-start(), calls=%async_computation.25 | async-start | bytes 1310720 | tf_op jit(solution)/shard_map/all_gather | solution.py:12
  637.8 31.7 %all-to-all-start.5 = ((f32[8,256,128]{1,2,0:T(8,128)}), f32[8,256,128]{1,2,0:T(8,128)S(1)}, u32[]{:S(2)}, u32[]{:S(2)}) async-start(f32[8,256,128]{1,2,0:T(8,128)} %copy.47), calls=%async_computation.10 | async-start | bytes 2097152 | tf_op jit(solution)/shard_map/all_to_all | solution.py:13
  643.3 97.8 %reduce-scatter.19.cloned.1.call-start = ((), (), s32[]{:S(2)}) async-start(), calls=%async_computation.26 | async-start | bytes 2359296 | tf_op jit(solution)/shard_map/reduce_scatter | solution.py:29
  675.1 83.9 %all-gather.20.cloned.1.call-start = ((), (), s32[]{:S(2)}) async-start(), calls=%async_computation.27 | async-start | bytes 1310720 | tf_op jit(solution)/shard_map/all_gather | solution.py:12
  742.8 119.5 %reduce-scatter.21.cloned.1.call-start = ((), (), s32[]{:S(2)}) async-start(), calls=%async_computation.28 | async-start | bytes 2359296 | tf_op jit(solution)/shard_map/reduce_scatter | solution.py:33
  796.1 83.5 %all-gather.22.cloned.1.call-start = ((), (), s32[]{:S(2)}) async-start(), calls=%async_computation.29 | async-start | bytes 1310720 | tf_op jit(solution)/shard_map/all_gather | solution.py:12
  862.4 541.1 %reduce-scatter.23.cloned.1.call-start = ((), (), s32[]{:S(2)}) async-start(), calls=%async_computation.30 | async-start | bytes 28311552 | tf_op jit(solution)/shard_map/reduce_scatter | solution.py:42
  1000.7 2.4 copy-start
Sparse Core Ops, SparseCore 0:
  10.1 19.4 all-gather.23
  65.9 66.3 reduce-scatter.8
  133.9 15.7 all-gather.9
  187.0 65.9 reduce-scatter.10
  255.0 15.7 all-gather.11
  307.9 66.1 reduce-scatter.12
  375.6 15.8 all-gather.13
  430.8 65.8 reduce-scatter.14
  498.8 15.7 all-gather.15
  551.7 66.1 reduce-scatter.16
  619.5 15.6 all-gather.17
  675.3 65.8 reduce-scatter.18
  743.3 15.7 all-gather.19
  796.2 66.1 reduce-scatter.20
  863.8 15.7 all-gather.21
  1000.8 402.6 reduce-scatter.22
where the time goes:
time: 1430 us; the launch traced here: 1420 us
  waiting for transfers between devices  1030 us (72%)
  blocking collectives  195 us (14%)
  matrix products  131 us (9%)
  local copies, waits for them, and re-layouts  22.8 us (2%)
  between operations  14.5 us (1%)
    reduce_scatter x1, waiting for transfers between devices, shards(): lax.psum_scatter(jnp.einsum('tajb,jbm->mta', trailing_factor, stacked, pr...  392 us
    reduce_scatter x4, waiting for transfers between devices, shards(): lax.psum_scatter(product(inverse_blocks[j], reduced_spread), 'col', scatt...  265 us
    reduce_scatter x3, waiting for transfers between devices, shards(): lax.psum_scatter(partial_value, 'col', scatter_dimension=1, tiled=True)  197 us
    all_to_all x6, blocking collectives, remap(): lax.all_to_all(full, 'col', split_axis=0, concat_axis=1, tiled=True)  189 us
    all_gather x8, waiting for transfers between devices, remap(): full = lax.all_gather(block, 'row', axis=0, tiled=True)  138 us
    dot_general x1, matrix products, shards(): jnp.einsum('tajb,jbm->mta', trailing_factor, stacked, precision=lax.Preci...  86.8 us
    dot_general x10, matrix products, product(): jnp.dot(left, right, precision=lax.Precision.HIGHEST, preferred_element_t...  44.3 us
    all_to_all x2, waiting for transfers between devices, remap(): lax.all_to_all(full, 'col', split_axis=0, concat_axis=1, tiled=True)  39.2 us
  transfers between devices with their start and end apart: 18, of which 18 were waited for; matrix products, arithmetic and copies ran while one was open for 1% of the time, Pallas kernels for 0%

commit v1 on v0

v1 whole, which is shorter than its diff:
```python
import functools

import jax
import jax.numpy as jnp
from jax import lax
from jax.experimental import pallas as pl
from jax.experimental.pallas import tpu as pltpu
from jax.sharding import PartitionSpec as P


def trailing_update(trailing_factor, trailing_columns, own, other, kept, got):
    cols = lax.axis_size("col")
    h = lax.rem(lax.axis_index("col"), 2)
    trail, rows, _, _ = trailing_factor.shape
    half = rows // 2
    width = trailing_columns.shape[2]
    groups = [[2 * g + p for g in range(cols // 2)] for p in range(2)]
    partial = contract(kept, own) + contract(got, other)
    summed = lax.psum_scatter(
        partial, "col", scatter_dimension=2, axis_index_groups=groups, tiled=True
    )
    mine = lax.dynamic_slice_in_dim(summed, h * width, width, 2)
    theirs = lax.dynamic_slice_in_dim(summed, (1 - h) * width, width, 2)
    back = lax.ppermute(theirs, "col", swaps(cols))
    low = jnp.where(h == 0, mine, back)
    high = jnp.where(h == 0, back, mine)
    return trailing_columns - jnp.concatenate([low, high], axis=1)


def contract(factor, solved):
    return jnp.einsum(
        "tajb,jbm->tam",
        factor,
        solved,
        precision=lax.Precision.HIGH,
        preferred_element_type=jnp.float32,
    )


def swaps(cols):
    return [(c, c ^ 1) for c in range(cols)]


def swap_factor(trailing_factor):
    cols = lax.axis_size("col")
    h = lax.rem(lax.axis_index("col"), 2)
    half = trailing_factor.shape[1] // 2
    kept = lax.dynamic_slice_in_dim(trailing_factor, h * half, half, 1)
    sent = lax.dynamic_slice_in_dim(trailing_factor, (1 - h) * half, half, 1)
    return kept, lax.ppermute(sent, "col", swaps(cols))


def split(value):
    high = value.astype(jnp.bfloat16)
    low = (value - high.astype(jnp.float32)).astype(jnp.bfloat16)
    return high, low


def dot3(left, right):
    left_high, left_low = split(left)
    right_high, right_low = split(right)

    def one(a, b):
        return jnp.dot(a, b, preferred_element_type=jnp.float32)

    return one(left_high, right_high) + (one(left_high, right_low) + one(left_low, right_high))


def chain_kernel(
    R, C, steps, panel, inverse, columns, solved_out, whitened_out,
    blocks, wants, held, parts, stage, acc, kept,
    own_sem, swap_send, swap_recv, want_send, want_recv, want_own, part_send, part_recv,
    root_send, fork_send, held_recv, piece_send, piece_recv, out_sem,
):
    pairs = panel.shape[0]
    G = C // 2
    Q = G
    rows = blocks.shape[2]
    lag = 2
    r = lax.axis_index("row")
    c = lax.axis_index("col")
    g = c // 2
    h = lax.rem(c, 2)
    is_root = r == g
    is_lead = lax.rem(r, 2) == lax.rem(g, 2)
    sibling = r + 1 - 2 * lax.rem(r, 2)

    def remote(src, dst, send, recv, row, col):
        return pltpu.make_async_remote_copy(
            src_ref=src, dst_ref=dst, send_sem=send, recv_sem=recv,
            device_id=(row, col), device_id_type=pl.DeviceIdType.MESH,
        )

    def mine(src, dst, sem):
        return pltpu.make_async_copy(src, dst, sem)

    barrier = pltpu.get_barrier_semaphore()
    for o in range(1, C):
        pl.semaphore_signal(
            barrier, inc=1, device_id=(r, lax.rem(c + o, C)), device_id_type=pl.DeviceIdType.MESH
        )
    for o in range(1, R):
        for p in range(2):
            pl.semaphore_signal(
                barrier, inc=1, device_id=(lax.rem(r + o, R), 2 * g + p),
                device_id_type=pl.DeviceIdType.MESH,
            )
    pl.semaphore_wait(barrier, C - 1 + 2 * (R - 1))

    def want_copy(p):
        return remote(
            columns.at[:, pl.ds(p * rows, rows), :], wants.at[c], want_send.at[p], want_recv.at[c],
            r, 2 * r + p,
        )

    def want_mine(p):
        return mine(columns.at[:, pl.ds(p * rows, rows), :], wants.at[c], want_own)

    for p in range(2):
        here = c == 2 * r + p

        @pl.when(jnp.logical_not(here))
        def _():
            want_copy(p).start()

        @pl.when(here)
        def _():
            want_mine(p).start()

    def block_of(s, i):
        j = s // 2
        return jnp.where(lax.rem(s, 2) == 1, pairs + j, j * (j - 1) // 2 + i)

    def count_of(s):
        return jnp.where(lax.rem(s, 2) == 1, 1, s // 2)

    def each_block(k, action):
        @pl.when(k < pairs)
        def _():
            action(panel, k)

        @pl.when(k >= pairs)
        def _():
            action(inverse, k - pairs)

    def start_blocks(s):
        def body(i, _):
            k = block_of(s, i)

            def action(source, at):
                mine(
                    source.at[at, pl.ds(pl.multiple_of(h * rows, rows), rows), :],
                    blocks.at[k, h], own_sem.at[k],
                ).start()
                remote(
                    source.at[at, pl.ds(pl.multiple_of((1 - h) * rows, rows), rows), :],
                    blocks.at[k, h], swap_send.at[k], swap_recv.at[k], r, 2 * g + 1 - h,
                ).start()

            each_block(k, action)
            return 0

        lax.fori_loop(0, count_of(s), body, 0)

    def swapped(k):
        return remote(
            blocks.at[k, h], blocks.at[k, 1 - h], swap_send.at[k], swap_recv.at[k], r, 2 * g + 1 - h
        )

    def wait_blocks(s):
        def body(i, _):
            k = block_of(s, i)
            mine(blocks.at[k, h], blocks.at[k, h], own_sem.at[k]).wait()
            swapped(k).wait_recv()
            return 0

        lax.fori_loop(0, count_of(s), body, 0)

    def chunk(s, half, q):
        return held.at[s, half, pl.ds(2 * q, 2)]

    def part_copy(s, q, up):
        step = 1 if up else -1
        return remote(
            stage.at[q], parts.at[1 if up else 0, s - 1, q], part_send.at[q],
            part_recv.at[1 if up else 0, s - 1, q], r, 2 * (g + step) + h,
        )

    def root_copy(s, q, o):
        return remote(
            chunk(s, h, q), chunk(s, h, q), root_send.at[q, o - 1], held_recv.at[s, h, q],
            lax.rem(r + 2 * o, R), c,
        )

    def fork_copy(s, q, n):
        half = h if n < 2 else 1 - h
        row, col = (r, 2 * g + 1 - h) if n == 0 else (sibling, c)
        return remote(
            chunk(s, half, q), chunk(s, half, q), fork_send.at[q, n], held_recv.at[s, half, q],
            row, col,
        )

    def piece_copy(s, q, p):
        return remote(
            held.at[s, h, 2 * q + p], kept.at[s // 2, h], piece_send.at[q, p],
            piece_recv.at[s // 2, h], r, 2 * q + p,
        )

    def pieces(s, q, action):
        for p in range(2):
            @pl.when(2 * q + p != c)
            def _():
                action(piece_copy(s, q, p))

    def finish_root(s, q):
        @pl.when(s >= 1)
        def _():
            for o in range(1, R // 2):
                root_copy(s, q, o).wait_send()

        for o in range(1, R // 2):
            root_copy(s, q, o).start()

        @pl.when(lax.rem(s, 2) == 1)
        def _():
            @pl.when(s >= 3)
            def _():
                pieces(s, q, lambda copy: copy.wait_send())

            pieces(s, q, lambda copy: copy.start())
            for p in range(2):
                @pl.when(2 * q + p == c)
                def _():
                    kept[s // 2, h] = held[s, h, 2 * q + p]

    def first(s, q):
        @pl.when(s == 0)
        def _():
            @pl.when(is_root)
            def _():
                for p in range(2):
                    m = 2 * q + p

                    @pl.when(m != c)
                    def _():
                        remote(
                            wants.at[m], wants.at[m], want_send.at[0], want_recv.at[m], r, m
                        ).wait_recv()

                    @pl.when(m == c)
                    def _():
                        mine(wants.at[m], wants.at[m], want_own).wait()

                    held[0, h, m] = wants[m, 0]
                finish_root(s, q)

        @pl.when(s >= 1)
        def _():
            @pl.when(q == 0)
            def _():
                wait_blocks(s)

                @pl.when(s + 2 < 2 * steps)
                def _():
                    start_blocks(s + 2)

            acc[...] = jnp.zeros_like(acc)

            def body(i, _):
                k = block_of(s, i)
                source = jnp.where(lax.rem(s, 2) == 1, s - 1, 2 * i + 1)
                for half in range(2):
                    left = blocks[k, half]
                    for p in range(2):
                        acc[p] += dot3(left, held[source, half, 2 * q + p])
                return 0

            lax.fori_loop(0, count_of(s), body, 0)

            @pl.when((g >= r) & (g < G - 1))
            def _():
                remote(
                    stage.at[q], parts.at[0, s - 1, q], part_send.at[q], part_recv.at[0, s - 1, q],
                    r, 2 * jnp.maximum(g - 1, 0) + h,
                ).wait_recv()
                acc[...] += parts[0, s - 1, q]

            @pl.when((g <= r) & (g > 0))
            def _():
                remote(
                    stage.at[q], parts.at[1, s - 1, q], part_send.at[q], part_recv.at[1, s - 1, q],
                    r, 2 * jnp.minimum(g + 1, G - 1) + h,
                ).wait_recv()
                acc[...] += parts[1, s - 1, q]

            for up in (False, True):
                @pl.when((g < r) if up else (g > r))
                def _():
                    @pl.when(s >= 2)
                    def _():
                        part_copy(s, q, up).wait_send()

                    stage[q] = acc[...]
                    part_copy(s, q, up).start()

            @pl.when(is_root)
            def _():
                @pl.when(lax.rem(s, 2) == 1)
                def _():
                    for p in range(2):
                        held[s, h, 2 * q + p] = acc[p]

                @pl.when(lax.rem(s, 2) == 0)
                def _():
                    for p in range(2):
                        held[s, h, 2 * q + p] = wants[2 * q + p, s // 2] - acc[p]

                finish_root(s, q)

    def arrived(s, half, q):
        remote(
            chunk(s, half, q), chunk(s, half, q), root_send.at[0, 0], held_recv.at[s, half, q],
            sibling, c,
        ).wait_recv()

    def second(s, q):
        @pl.when(jnp.logical_not(is_root))
        def _():
            arrived(s, h, q)

        @pl.when(is_lead)
        def _():
            @pl.when(s >= 1)
            def _():
                for n in range(3):
                    fork_copy(s, q, n).wait_send()

            fork_copy(s, q, 0).start()
            fork_copy(s, q, 1).start()

        arrived(s, 1 - h, q)

        @pl.when(is_lead)
        def _():
            fork_copy(s, q, 2).start()

    start_blocks(jnp.int32(1))
    start_blocks(jnp.int32(2))
    total = 2 * steps * Q

    def turn(t, _):
        @pl.when(t < total)
        def _():
            first(t // Q, lax.rem(t, Q))

        @pl.when(t >= lag)
        def _():
            second((t - lag) // Q, lax.rem(t - lag, Q))

        return 0

    lax.fori_loop(0, total + lag, turn, 0)

    for j in range(steps):
        mine(held.at[2 * j + 1], solved_out.at[j], out_sem.at[j]).start()

    last = jnp.int32(2 * steps - 1)

    def drain(q, _):
        @pl.when(is_root)
        def _():
            for o in range(1, R // 2):
                root_copy(last, q, o).wait_send()
            pieces(last, q, lambda copy: copy.wait_send())

        @pl.when(is_lead)
        def _():
            for n in range(3):
                fork_copy(last, q, n).wait_send()

        for up in (False, True):
            @pl.when((g < r) if up else (g > r))
            def _():
                part_copy(last, q, up).wait_send()

        return 0

    lax.fori_loop(0, Q, drain, 0)

    def drain_block(k, _):
        swapped(k).wait_send()
        return 0

    lax.fori_loop(0, pairs + steps, drain_block, 0)
    for p in range(2):
        @pl.when(c != 2 * r + p)
        def _():
            want_copy(p).wait_send()

            for j in range(steps):
                remote(
                    kept.at[j, p], kept.at[j, p], piece_send.at[0, 0], piece_recv.at[j, p],
                    r, 2 * r + p,
                ).wait_recv()

    done = mine(kept, whitened_out, out_sem.at[steps])
    done.start()
    for j in range(steps):
        mine(held.at[2 * j + 1], solved_out.at[j], out_sem.at[j]).wait()
    done.wait()


def solve_chain(panel, inverse_blocks, columns):
    R = lax.axis_size("row")
    C = lax.axis_size("col")
    G = C // 2
    Q = G
    pairs = panel.shape[0]
    steps, height, width = columns.shape
    rows = height // 2
    depth = panel.shape[2]
    dma = pltpu.SemaphoreType.DMA
    f32 = jnp.float32
    flops = 6 * 2 * rows * (2 * depth) * C * width * (pairs + steps)
    solved, whitened = pl.pallas_call(
        functools.partial(chain_kernel, R, C, steps),
        out_shape=(
            jax.ShapeDtypeStruct((steps, 2, C, rows, width), f32),
            jax.ShapeDtypeStruct((steps, 2, rows, width), f32),
        ),
        in_specs=[pl.BlockSpec(memory_space=pl.ANY)] * 3,
        out_specs=(pl.BlockSpec(memory_space=pl.ANY), pl.BlockSpec(memory_space=pl.ANY)),
        scratch_shapes=[
            pltpu.VMEM((pairs + steps, 2, rows, depth), f32),
            pltpu.VMEM((C, steps, rows, width), f32),
            pltpu.VMEM((2 * steps, 2, C, rows, width), f32),
            pltpu.VMEM((2, 2 * steps - 1, Q, 2, rows, width), f32),
            pltpu.VMEM((Q, 2, rows, width), f32),
            pltpu.VMEM((2, rows, width), f32),
            pltpu.VMEM((steps, 2, rows, width), f32),
            dma((pairs + steps,)),
            dma((pairs + steps,)),
            dma((pairs + steps,)),
            dma((2,)),
            dma((C,)),
            dma,
            dma((Q,)),
            dma((2, 2 * steps - 1, Q)),
            dma((Q, max(R // 2 - 1, 1))),
            dma((Q, 3)),
            dma((2 * steps, 2, Q)),
            dma((Q, 2)),
            dma((steps, 2)),
            dma((steps + 1,)),
        ],
        compiler_params=pltpu.CompilerParams(
            collective_id=0, has_side_effects=True, vmem_limit_bytes=56 * 1024 * 1024
        ),
        cost_estimate=pl.CostEstimate(
            flops=flops * 10, bytes_accessed=400 * 1024 * 1024, transcendentals=0
        ),
    )(panel, inverse_blocks, columns)
    return solved, whitened.reshape(steps, height, width)


def shards(panel, inverse_blocks, trailing_factor, columns, trailing_columns):
    steps, height, _ = columns.shape
    order = height * lax.axis_size("row")
    kept, got = swap_factor(trailing_factor)
    solved, whitened = solve_chain(panel, inverse_blocks, columns)
    h = lax.rem(lax.axis_index("col"), 2)
    rows = solved.shape[3]

    def half(p):
        part = lax.dynamic_index_in_dim(solved, p, 1, keepdims=False)
        return jnp.transpose(part, (0, 2, 1, 3)).reshape(steps, rows, -1)

    updated = trailing_update(
        trailing_factor, trailing_columns, half(h), half(1 - h), kept, got
    )
    local_squares = jnp.sum(whitened * whitened, axis=(0, 1))
    variance_drop = lax.psum(local_squares, "row") / (steps * order)
    return (whitened, updated, variance_drop)


def solution(mesh):
    return jax.shard_map(
        shards,
        mesh=mesh,
        in_specs=(
            P(None, "row", "col"),
            P(None, "row", "col"),
            P(None, "row", None, "col"),
            P(None, "row", "col"),
            P(None, "row", "col"),
        ),
        out_specs=(P(None, "row", "col"), P(None, "row", "col"), P("col")),
        check_vma=False,
    )
```

time: 1430 us -> 1100 us (0.77)
  waiting for transfers between devices: 1030 us -> 253 us
  Pallas kernels: 0 us -> 707 us
  blocking collectives: 195 us -> 6.75 us
  matrix products: 131 us -> 49.6 us
  local copies, waits for them, and re-layouts: 22.8 us -> 58.8 us
    pallas_call x0 -> x1, Pallas kernels: none -> 707 us  [solve_chain(): pl.pallas_call(functools.partial(chain_kernel, R, C, steps), out_shape=(j...]
    reduce_scatter x8 -> x1, waiting for transfers between devices: 853 us -> 226 us  [trailing_update(): lax.psum_scatter(partial, 'col', scatter_dimension=2, axis_index_groups=g...]
    all_to_all x6 -> x0, blocking collectives: 189 us -> none  [remap(): lax.all_to_all(full, 'col', split_axis=0, concat_axis=1, tiled=True)]
    all_gather x8 -> x0, waiting for transfers between devices: 138 us -> none  [remap(): full = lax.all_gather(block, 'row', axis=0, tiled=True)]
    dot_general x11 -> x2, matrix products: 131 us -> 49.6 us  [contract(): jnp.einsum('tajb,jbm->tam', factor, solved, precision=lax.Precision.HIGH,...]
    all_to_all x2 -> x0, waiting for transfers between devices: 39.2 us -> none  [remap(): lax.all_to_all(full, 'col', split_axis=0, concat_axis=1, tiled=True)]
    ppermute x0 -> x2, waiting for transfers between devices: none -> 27.3 us  [the longest x1 27.3 us: trailing_update(): back = lax.ppermute(theirs, 'col', swaps(cols))]
    dynamic_slice x0 -> x2, local copies, waits for them, and re-layouts: none -> 19.7 us  [the longest x1 18.2 us: swap_factor(): sent = lax.dynamic_slice_in_dim(trailing_factor, (1 - h) * half, half, 1)]
  transfers between devices with their start and end apart: 18 -> 3, of which waited for: 18 -> 2; matrix products, arithmetic and copies ran while one was open for 1% -> 5% of each run, Pallas kernels for 0% -> 64%
where the time goes in v1:
time: 1100 us
  Pallas kernels  707 us (64%)
  waiting for transfers between devices  253 us (23%)
  local copies, waits for them, and re-layouts  58.8 us (5%)
  matrix products  49.6 us (5%)
  between operations  14.1 us (1%)
    pallas_call x1, Pallas kernels, solve_chain(): pl.pallas_call(functools.partial(chain_kernel, R, C, steps), out_shape=(j...  707 us
    reduce_scatter x1, waiting for transfers between devices, trailing_update(): lax.psum_scatter(partial, 'col', scatter_dimension=2, axis_index_groups=g...  226 us
    dot_general x2, matrix products, contract(): jnp.einsum('tajb,jbm->tam', factor, solved, precision=lax.Precision.HIGH,...  49.6 us
    ppermute x1, waiting for transfers between devices, trailing_update(): back = lax.ppermute(theirs, 'col', swaps(cols))  27.3 us
  transfers between devices with their start and end apart: 3, of which 2 were waited for; matrix products, arithmetic and copies ran while one was open for 5% of the time, Pallas kernels for 64%

profile of v1, /device:TPU:0, one launch (start us, length us, event | category | flops | bytes accessed | tf_op | source)
XLA Modules:
  0.0 1099.0 jit_solution(1182913133159408519)
XLA Ops:
  7.2 0.0 reduce-scatter.2.cloned.1.call-start
  7.2 18.2 %constant_dynamic-slice_fusion.1 = (f32[12,256,4,256]{3,2,1,0:T(4,128)}, f32[12,256,4,256]{3,2,1,0:T(4,128)}) fusion(f32[12,512,4,256]{3,2,1,0:T(4,128)} %param.7, s32[]{:T(128)S(6)} %select_n.34, s32[]{:T(128)S(6)} %select_n.32), kind=kLoop, calls=%fused_computation.10 | loop fusion | bytes 50331656 | tf_op jit(solution)/shard_map/dynamic_slice | solution.py:49
  25.4 11.2 %copy.17 = f32[12,256,4,256]{3,1,2,0:T(8,128)} copy(f32[12,256,4,256]{3,2,1,0:T(4,128)} %get-tuple-element.7) | data formatting | bytes 25165824
  36.6 3.0 collective-permute-start
  39.6 706.7 %shard_map.76 = (f32[4,2,8,256,128]{4,3,2,1,0:T(8,128)}, f32[4,2,256,128]{3,2,1,0:T(8,128)}) custom-call(f32[6,512,256]{2,1,0:T(8,128)} %panel.1, f32[4,512,256]{2,1,0:T(8,128)} %inverse.1, f32[4,512,128]{2,1,0:T(8,128)} %columns.1), custom_call_target="tpu_custom_call" | custom-call | flops 161061273600 | bytes 419430400 | tf_op jit(solution)/shard_map/pallas_call | solution.py:425
  746.3 6.2 dynamic-slice_bitcast_fusion
  752.5 4.4 copy.11
  756.8 4.9 reshape.18
  761.7 6.6 copy.13
  768.4 4.9 reshape.20
  773.2 0.0 copy-start
  773.2 25.5 %fusion = f32[12,256,1024,1]{2,1,3,0:T(8,128)S(1)} fusion(f32[4,256,1024,1]{2,1,0,3:T(8,128)} %reshape.18, f32[12,256,4,256]{3,2,1,0:T(4,128)} %get-tuple-element.8), kind=kOutput, calls=%fused_computation | convolution fusion | flops 19327352832 | bytes 29360128 | tf_op jit(solution)/shard_map/tajb,jbm->tam/dot_general | solution.py:31
  798.8 0.0 collective-permute-done
  798.8 0.0 copy-done
  798.8 24.1 %bitcast_add_fusion = f32[12,256,1024]{2,1,0:T(8,128)} fusion(f32[12,256,1024,1]{2,1,3,0:T(8,128)S(1)} %fusion, f32[12,256,4,256]{3,1,2,0:T(8,128)} %collective-permute-done, f32[4,256,1024,1]{2,1,0,3:T(8,128)S(1)} %copy-done), kind=kOutput, calls=%fused_computation.2 | convolution fusion | flops 19330498560 | bytes 41943040 | tf_op jit(solution)/shard_map/tajb,jbm->tam/dot_general | solution.py:31
  822.9 0.0 copy-start.1
  822.9 0.0 reduce-scatter.2.cloned.1.call-update
  822.9 226.2 %reduce-scatter.2.cloned.1.call-done = f32[12,256,256]{2,1,0:T(8,128)} async-done(((f32[12,256,1024]{2,1,0:T(8,128)}), f32[12,256,256]{2,1,0:T(8,128)}) %reduce-scatter.2.cloned.1.call-update) | async-done | bytes 3145744 | tf_op jit(solution)/shard_map/reduce_scatter | solution.py:19
  1049.1 1.5 constant_dynamic-slice_fusion
  1050.6 1.5 collective-permute-start.1
  1052.2 0.0 copy-done.1
  1052.2 0.3 multiply_reduce_fusion
  1052.4 6.7 psum.7
  1059.2 0.0 copy-start.2
  1059.2 0.5 broadcast_multiply_fusion
  1059.7 27.3 %collective-permute-done.1 = f32[12,256,128]{2,1,0:T(8,128)} collective-permute-done((f32[12,256,128]{2,1,0:T(8,128)S(1)}, f32[12,256,128]{2,1,0:T(8,128)}, u32[]{:S(2)}, u32[]{:S(2)}) %collective-permute-start.1) | collective-permute-done | bytes 1572896 | tf_op jit(solution)/shard_map/ppermute | solution.py:24
  1087.0 2.1 dynamic-slice_select_fusion.1
  1089.2 0.0 copy-done.2
  1089.2 2.0 maximum_subtract_fusion
  1091.2 1.0 copy.21
Async XLA Ops:
  7.2 1041.9 %reduce-scatter.2.cloned.1.call-start = ((), (), s32[]{:S(2)}) async-start(), calls=%async_computation.1 | async-start | bytes 15728640 | tf_op jit(solution)/shard_map/reduce_scatter | solution.py:19
  36.6 762.2 %collective-permute-start = (f32[12,256,4,256]{3,1,2,0:T(8,128)}, f32[12,256,4,256]{3,1,2,0:T(8,128)}, u32[]{:S(2)}, u32[]{:S(2)}) collective-permute-start(f32[12,256,4,256]{3,1,2,0:T(8,128)} %copy.17), channel_id=1, source_target_pairs={{0,1},{1,0},{2,3},{3,2},{4,5},{5,4},{6,7},{7,6},{8,9},{9,8},{10,11... | collective-permute-start | bytes 37748744 | tf_op jit(solution)/shard_map/ppermute | solution.py:50
  773.2 25.6 %copy-start = (f32[4,256,1024,1]{2,1,0,3:T(8,128)S(1)}, f32[4,256,1024,1]{2,1,0,3:T(8,128)}, u32[]{:S(2)}) copy-start(f32[4,256,1024,1]{2,1,0,3:T(8,128)} %reshape.20) | copy-start | bytes 12582916
  822.9 229.2 %copy-start.1 = (f32[4,2,256,128]{3,2,1,0:T(8,128)S(1)}, f32[4,2,256,128]{3,2,1,0:T(8,128)}, u32[]{:S(2)}) copy-start(f32[4,2,256,128]{3,2,1,0:T(8,128)} %get-tuple-element.5) | copy-start | bytes 3145732
  1050.6 36.4 %collective-permute-start.1 = (f32[12,256,128]{2,1,0:T(8,128)S(1)}, f32[12,256,128]{2,1,0:T(8,128)}, u32[]{:S(2)}, u32[]{:S(2)}) collective-permute-start(f32[12,256,128]{2,1,0:T(8,128)S(1)} %constant_dynamic-slice_fusion), channel_id=1, source_target_pairs={{0,1},{1,0},{2,3},{3,2},{4,5},{5,4},{6,7},{7,6},{8,9},{9,8},{10,11... | collective-permute-start | bytes 4718600 | tf_op jit(solution)/shard_map/ppermute | solution.py:24
  1059.2 30.0 %copy-start.2 = (f32[12,512,128]{2,1,0:T(8,128)S(1)}, f32[12,512,128]{2,1,0:T(8,128)}, u32[]{:S(2)}) copy-start(f32[12,512,128]{2,1,0:T(8,128)} %param.9) | copy-start | bytes 9437188
Sparse Core Ops, SparseCore 0:
  823.1 225.9 reduce-scatter.1
